TPU v7x, 768 devices: a whole 4x8x12 slice. The times are simulated.
768 devices in a mesh: blk: 192 (over z, x, y_lo, core), group: 4 (over y_hi).
Axes of the slice: x: 4, y: 8 (y_hi: 4, y_lo: 2; y = y_hi * 2 + y_lo), z: 12, core: 2. Of those that a mesh axis runs over, the one named last changes fastest.
Arguments:
- audio_embed: bfloat16 [196608, 768], P(('blk', 'group')), may hold values from -0.19921875 to 0.19921875
- text_embed: bfloat16 [196608, 768], P(('blk', 'group')), may hold values from -0.19921875 to 0.19921875
- caption_ids: int32 [196608], P(('blk', 'group')), may hold values from 0 to 4095
- pairing: int32 [4], replicated, may hold values from 0 to 3, each once
- logit_scale: float32 [1], replicated, may hold values from 3 to 15
- logit_bias: float32 [1], replicated, may hold values from -4 to 0
Outputs:
- loss: float32 [], replicated
- grad_audio: bfloat16 [196608, 768], P(('blk', 'group'))
- grad_text: bfloat16 [196608, 768], P(('blk', 'group'))
Inputs may be any that keep to these rules, and one draw needn't show every extreme that they name: `pairing`: a permutation of the group indices.
All inputs are finite; a program needn't handle non-finite values.
Results may differ from a plain program's by a relative error of at most 0.0011.
The roundings to bfloat16 on the way count: a program that leaves them out, or rounds other values in their place, can miss the bound.
Values may be sent and summed in bfloat16 or wider, within the bound.
No kernel may reach another device: no remote copies, remote signals or barrier semaphores. Data moves between devices by JAX's collectives and lax.ppermute only.
A program may use at most 32 MiB of HBM per device.

v0:
```python
import jax
import jax.numpy as jnp
from jax import lax
from jax.sharding import PartitionSpec as P

ROUNDS = 4


def shifted(array, axis, by):
    count = lax.axis_size(axis)
    return lax.ppermute(array, axis, [(i, (i + by) % count) for i in range(count)])


def block_terms(audio, audio_ids, text, text_ids, scale, bias):
    dots = lax.dot_general(
        audio, text, (((1,), (1,)), ((), ())), preferred_element_type=jnp.float32
    )
    logits = scale * dots + bias
    sign = jnp.where(audio_ids[:, None] == text_ids[None, :], 1.0, -1.0).astype(jnp.float32)
    margin = sign * logits
    total = jnp.sum(jax.nn.softplus(-margin))
    coeff = (-scale * sign * jax.nn.sigmoid(-margin)).astype(jnp.bfloat16)
    grad_a = jnp.dot(coeff, text, preferred_element_type=jnp.float32)
    grad_t = lax.dot_general(
        coeff, audio, (((0,), (0,)), ((), ())), preferred_element_type=jnp.float32
    )
    return (total, grad_a, grad_t)


def body(audio_embed, text_embed, caption_ids, pairing, logit_scale, logit_bias):
    rows = audio_embed.shape[0]
    width = audio_embed.shape[1]
    scale = logit_scale[0]
    bias = logit_bias[0]
    mine = lax.axis_index("group")
    target = pairing[mine]
    pair_count = rows * lax.axis_size("blk") * lax.axis_size("group")
    loss_total, grad_audio, grad_text = block_terms(
        audio_embed, caption_ids, text_embed, caption_ids, scale, bias
    )
    moving_text = text_embed
    moving_ids = caption_ids
    carried = jnp.zeros((rows, width), jnp.float32)
    for step in range(ROUNDS):
        moving_text, moving_ids = shifted((moving_text, moving_ids), "blk", 1)
        total, grad_a, grad_t = block_terms(
            audio_embed, caption_ids, moving_text, moving_ids, scale, bias
        )
        loss_total = loss_total + total
        grad_audio = grad_audio + grad_a
        if step == 0:
            carried = grad_t
        else:
            carried = shifted(carried, "blk", 1) + grad_t
    returned = shifted(carried, "blk", -ROUNDS)
    grad_text = grad_text + returned
    piece_text = lax.all_gather(text_embed, "group", axis=0, tiled=True)
    piece_ids = lax.all_gather(caption_ids, "group", axis=0, tiled=True)
    count = piece_text.shape[0] // rows
    owners = jnp.arange(count)
    keep = owners == target
    text_part = jnp.sum(
        jnp.where(
            keep[:, None, None], piece_text.reshape(count, rows, width), jnp.zeros((), jnp.bfloat16)
        ),
        axis=0,
    )
    ids_part = jnp.sum(jnp.where(keep[:, None], piece_ids.reshape(count, rows), 0), axis=0).astype(
        jnp.int32
    )
    partner_loss, partner_ga, partner_gt = block_terms(
        audio_embed, caption_ids, text_part, ids_part, scale, bias
    )
    loss_total = loss_total + partner_loss
    grad_audio = grad_audio + partner_ga
    piece = lax.all_gather(partner_gt, "group", axis=0, tiled=True)
    count = piece.shape[0] // rows
    owners = jnp.arange(count)
    keep = jnp.take(pairing, owners) == mine
    grad_text = grad_text + jnp.sum(
        jnp.where(keep[:, None, None], piece.reshape(count, rows, width), 0.0), axis=0
    )
    loss = lax.psum(loss_total, ("blk", "group")) / jnp.float32(pair_count)
    return (loss, grad_audio.astype(jnp.bfloat16), grad_text.astype(jnp.bfloat16))


def solution(mesh):
    placed = (
        P(("blk", "group"), None),
        P(("blk", "group"), None),
        P(("blk", "group")),
        P(),
        P(),
        P(),
    )
    return jax.shard_map(
        body,
        mesh=mesh,
        in_specs=placed,
        out_specs=(P(), P(("blk", "group"), None), P(("blk", "group"), None)),
        check_vma=False,
    )
```

profile of v0, /device:TPU:1, one launch (start us, length us, event | category | flops | bytes accessed | tf_op | source)
XLA Modules:
  0.0 308.0 jit_solution(12353606154075372017)
XLA Ops:
  7.2 0.7 all-gather.4.cloned.1.call-update
  8.0 4.6 %collective-permute-start = (s32[256]{0:T(256)}, s32[256]{0:T(256)S(1)}, u32[]{:S(2)}, u32[]{:S(2)}) collective-permute-start(s32[256]{0:T(256)} %param.8), channel_id=1, source_target_pairs={{0,4},{4,8},{8,12},{12,16},{16,20},{20,24},{24,28},{28,32},{32,36}... | collective-permute-start | bytes 3080 | tf_op jit(solution)/shard_map/ppermute | solution.py:11
  12.6 1.9 collective-permute-start.1
  14.5 1.2 dynamic_slice.3
  15.7 5.5 %collective-permute-done = s32[256]{0:T(256)S(1)} collective-permute-done((s32[256]{0:T(256)}, s32[256]{0:T(256)S(1)}, u32[]{:S(2)}, u32[]{:S(2)}) %collective-permute-start) | collective-permute-done | bytes 1056 | tf_op jit(solution)/shard_map/ppermute | solution.py:11
  21.2 1.9 collective-permute-start.2
  23.1 0.7 iota_compare_fusion
  23.8 6.9 %collective-permute-done.2 = s32[256]{0:T(256)S(1)} collective-permute-done((s32[256]{0:T(256)S(1)}, s32[256]{0:T(256)S(1)}, u32[]{:S(2)}, u32[]{:S(2)}) %collective-permute-start.2) | collective-permute-done | bytes 1056 | tf_op jit(solution)/shard_map/ppermute | solution.py:11
  30.7 1.9 collective-permute-start.4
  32.6 10.3 %all-gather = s32[4,1,256]{2,1,0:T(1,128)S(1)} all-gather(s32[1,1,256]{2,1,0:T(1,128)} %bitcast.53), channel_id=1, replica_groups=mesh['blk'=192,'group'=4] {'group'}, dimensions={0}, use_global_device_ids=true | all-gather | bytes 5120 | tf_op jit(solution)/shard_map/all_gather | solution.py:58
  42.9 1.9 collective-permute-start.6
  46.2 7.7 %collective-permute-done.6 = s32[256]{0:T(256)S(1)} collective-permute-done((s32[256]{0:T(256)S(1)}, s32[256]{0:T(256)S(1)}, u32[]{:S(2)}, u32[]{:S(2)}) %collective-permute-start.6) | collective-permute-done | bytes 1056 | tf_op jit(solution)/shard_map/ppermute | solution.py:11
  53.9 1.5 broadcast_compare_fusion
  55.6 9.5 %all-gather.4.cloned.1.call-done = bf16[1024,768]{1,0:T(8,128)(2,1)} async-done(((bf16[256,768]{1,0:T(8,128)(2,1)}), bf16[1024,768]{1,0:T(8,128)(2,1)}) %all-gather.4.cloned.1.call-update) | async-done | bytes 1572880 | tf_op jit(solution)/shard_map/all_gather | solution.py:57
  65.2 1.9 select_reduce_fusion.1
  67.1 1.1 fusion.31
  68.2 1.2 fusion.34
  69.5 1.1 fusion.27
  70.6 0.3 fusion.56
  70.9 3.9 %collective-permute-start.8 = (f32[256,768]{1,0:T(8,128)S(1)}, f32[256,768]{1,0:T(8,128)S(1)}, u32[]{:S(2)}, u32[]{:S(2)}) collective-permute-start(f32[256,768]{1,0:T(8,128)S(1)} %fusion.56), channel_id=1, source_target_pairs={{0,4},{4,8},{8,12},{12,16},{16,20},{20,24},{24,28},{28,32},{32,36}... | collective-permute-start | bytes 2359304 | tf_op jit(solution)/shard_map/ppermute | solution.py:11
  74.8 0.6 gather_fusion
  75.5 1.9 collective-permute-start.3
  77.4 0.6 fusion.33
  78.1 1.2 fusion.26
  79.3 8.6 %collective-permute-done.3 = bf16[256,768]{1,0:T(8,128)(2,1)} collective-permute-done((bf16[256,768]{1,0:T(8,128)(2,1)S(1)}, bf16[256,768]{1,0:T(8,128)(2,1)}, u32[]{:S(2)}, u32[]{:S(2)}) %collective-permute-start.3) | collective-permute-done | bytes 393248 | tf_op jit(solution)/shard_map/ppermute | solution.py:11
  87.9 4.5 %collective-permute-start.5 = (bf16[256,768]{1,0:T(8,128)(2,1)}, bf16[256,768]{1,0:T(8,128)(2,1)}, u32[]{:S(2)}, u32[]{:S(2)}) collective-permute-start(bf16[256,768]{1,0:T(8,128)(2,1)} %collective-permute-done.3), channel_id=1, source_target_pairs={{0,4},{4,8},{8,12},{12,16},{16,20},{20,24},{24,28},{28,32},{32,36}... | collective-permute-start | bytes 1179656 | tf_op jit(solution)/shard_map/ppermute | solution.py:11
  92.4 2.2 fusion.28
  94.6 0.3 convolution_add_fusion
  94.9 1.9 collective-permute-start.9
  96.9 0.3 fusion.40
  98.6 1.5 convolution_add_fusion.4
  100.1 23.2 %collective-permute-done.5 = bf16[256,768]{1,0:T(8,128)(2,1)} collective-permute-done((bf16[256,768]{1,0:T(8,128)(2,1)}, bf16[256,768]{1,0:T(8,128)(2,1)}, u32[]{:S(2)}, u32[]{:S(2)}) %collective-permute-start.5) | collective-permute-done | bytes 393248 | tf_op jit(solution)/shard_map/ppermute | solution.py:11
  123.3 4.4 %collective-permute-start.7 = (bf16[256,768]{1,0:T(8,128)(2,1)}, bf16[256,768]{1,0:T(8,128)(2,1)S(1)}, u32[]{:S(2)}, u32[]{:S(2)}) collective-permute-start(bf16[256,768]{1,0:T(8,128)(2,1)} %collective-permute-done.5), channel_id=1, source_target_pairs={{0,4},{4,8},{8,12},{12,16},{16,20},{20,24},{24,28},{28,32},{32,36}... | collective-permute-start | bytes 1179656 | tf_op jit(solution)/shard_map/ppermute | solution.py:11
  127.7 2.1 fusion.29
  129.8 21.5 %collective-permute-done.9 = f32[256,768]{1,0:T(8,128)S(1)} collective-permute-done((f32[256,768]{1,0:T(8,128)S(1)}, f32[256,768]{1,0:T(8,128)S(1)}, u32[]{:S(2)}, u32[]{:S(2)}) %collective-permute-start.9) | collective-permute-done | bytes 786464 | tf_op jit(solution)/shard_map/ppermute | solution.py:11
  151.3 1.2 fusion.51
  152.5 4.4 %collective-permute-start.10 = (f32[256,768]{1,0:T(8,128)}, f32[256,768]{1,0:T(8,128)}, u32[]{:S(2)}, u32[]{:S(2)}) collective-permute-start(f32[256,768]{1,0:T(8,128)} %fusion.51), channel_id=1, source_target_pairs={{0,4},{4,8},{8,12},{12,16},{16,20},{20,24},{24,28},{28,32},{32,36}... | collective-permute-start | bytes 2359304 | tf_op jit(solution)/shard_map/ppermute | solution.py:11
  156.9 1.4 convolution_add_fusion.3
  160.1 0.8 fusion.30
  162.2 1.4 convolution_add_fusion.2
  163.6 112.3 %psum.7 = f32[]{:T(128)} all-reduce(f32[]{:T(128)S(6)} %add.137), channel_id=1, replica_groups=mesh['blk'=192,'group'=4] {'blk','group'}, use_global_device_ids=true, to_apply=%region_8.9 | all-reduce | flops 1 | bytes 8 | tf_op jit(solution)/shard_map/psum | solution.py:83
  276.5 1.5 fusion.45
  278.0 3.8 %collective-permute-start.11 = (f32[256,768]{1,0:T(8,128)S(1)}, f32[256,768]{1,0:T(8,128)S(1)}, u32[]{:S(2)}, u32[]{:S(2)}) collective-permute-start(f32[256,768]{1,0:T(8,128)S(1)} %fusion.45), channel_id=1, source_target_pairs={{0,752},{4,756},{8,760},{12,764},{16,0},{20,4},{24,8},{28,12},{32,... | collective-permute-start | bytes 2359304 | tf_op jit(solution)/shard_map/ppermute | solution.py:11
  281.8 1.4 fusion.36
  283.3 1.1 fusion.1
  284.3 2.3 select_reduce_fusion
  286.6 12.3 %collective-permute-done.11 = f32[256,768]{1,0:T(8,128)S(1)} collective-permute-done((f32[256,768]{1,0:T(8,128)S(1)}, f32[256,768]{1,0:T(8,128)S(1)}, u32[]{:S(2)}, u32[]{:S(2)}) %collective-permute-start.11) | collective-permute-done | bytes 786464 | tf_op jit(solution)/shard_map/ppermute | solution.py:11
  298.9 1.1 add_convert_fusion
  (43 shorter events, 1.1 us)
Async XLA Ops:
  7.2 59.9 %copy-start = (bf16[256,768]{1,0:T(8,128)(2,1)S(1)}, bf16[256,768]{1,0:T(8,128)(2,1)}, u32[]{:S(2)}) copy-start(bf16[256,768]{1,0:T(8,128)(2,1)} %param.6) | copy-start | bytes 1179652
  7.2 58.0 %all-gather.4.cloned.1.call-start = ((), (), s32[]{:S(2)}) async-start(), calls=%async_computation | async-start | bytes 1966080 | tf_op jit(solution)/shard_map/all_gather | solution.py:57
  7.9 276.4 %all-gather.6.cloned.1.call-start = ((), (), s32[]{:S(2)}) async-start(), calls=%async_computation.1 | async-start | bytes 3932160 | tf_op jit(solution)/shard_map/all_gather | solution.py:76
  8.0 13.3 %collective-permute-start = (s32[256]{0:T(256)}, s32[256]{0:T(256)S(1)}, u32[]{:S(2)}, u32[]{:S(2)}) collective-permute-start(s32[256]{0:T(256)} %param.8), channel_id=1, source_target_pairs={{0,4},{4,8},{8,12},{12,16},{16,20},{20,24},{24,28},{28,32},{32,36}... | collective-permute-start | bytes 3080 | tf_op jit(solution)/shard_map/ppermute | solution.py:11
  12.6 56.9 %collective-permute-start.1 = (bf16[256,768]{1,0:T(8,128)(2,1)}, bf16[256,768]{1,0:T(8,128)(2,1)S(1)}, u32[]{:S(2)}, u32[]{:S(2)}) collective-permute-start(bf16[256,768]{1,0:T(8,128)(2,1)} %param.7), channel_id=1, source_target_pairs={{0,4},{4,8},{8,12},{12,16},{16,20},{20,24},{24,28},{28,32},{32,36}... | collective-permute-start | bytes 1179656 | tf_op jit(solution)/shard_map/ppermute | solution.py:11
  21.2 9.5 %collective-permute-start.2 = (s32[256]{0:T(256)S(1)}, s32[256]{0:T(256)S(1)}, u32[]{:S(2)}, u32[]{:S(2)}) collective-permute-start(s32[256]{0:T(256)S(1)} %collective-permute-done), channel_id=1, source_target_pairs={{0,4},{4,8},{8,12},{12,16},{16,20},{20,24},{24,28},{28,32},{32,36}... | collective-permute-start | bytes 3080 | tf_op jit(solution)/shard_map/ppermute | solution.py:11
  30.7 12.2 %collective-permute-start.4 = (s32[256]{0:T(256)S(1)}, s32[256]{0:T(256)S(1)}, u32[]{:S(2)}, u32[]{:S(2)}) collective-permute-start(s32[256]{0:T(256)S(1)} %collective-permute-done.2), channel_id=1, source_target_pairs={{0,4},{4,8},{8,12},{12,16},{16,20},{20,24},{24,28},{28,32},{32,36}... | collective-permute-start | bytes 3080 | tf_op jit(solution)/shard_map/ppermute | solution.py:11
  42.9 11.0 %collective-permute-start.6 = (s32[256]{0:T(256)S(1)}, s32[256]{0:T(256)S(1)}, u32[]{:S(2)}, u32[]{:S(2)}) collective-permute-start(s32[256]{0:T(256)S(1)} %collective-permute-done.4), channel_id=1, source_target_pairs={{0,4},{4,8},{8,12},{12,16},{16,20},{20,24},{24,28},{28,32},{32,36}... | collective-permute-start | bytes 3080 | tf_op jit(solution)/shard_map/ppermute | solution.py:11
  55.6 13.9 %copy-start.10 = (pred[256,256]{1,0:T(32,128)(4,1)}, pred[256,256]{1,0:T(32,128)(4,1)S(1)}, u32[]{:S(2)}) copy-start(pred[256,256]{1,0:T(32,128)(4,1)S(1)} %copy.85) | copy-start | bytes 196612
  55.6 13.9 %copy-start.9 = (s32[256]{0:T(256)S(1)}, s32[256]{0:T(256)}, u32[]{:S(2)}) copy-start(s32[256]{0:T(256)} %param.8) | copy-start | bytes 3076
  67.0 1.1 copy-start.3
  68.2 1.3 copy-start.12
  68.2 6.6 %copy-start.1 = (s32[4]{0:T(128)S(1)}, s32[4]{0:T(128)}, u32[]{:S(2)}) copy-start(s32[4]{0:T(128)} %param.9) | copy-start | bytes 52
  68.2 9.9 %copy-start.2 = (bf16[256,768]{1,0:T(8,128)(2,1)S(1)}, bf16[256,768]{1,0:T(8,128)(2,1)}, u32[]{:S(2)}) copy-start(bf16[256,768]{1,0:T(8,128)(2,1)} %param.7) | copy-start | bytes 1179652
  69.5 25.1 %copy-start.4 = (bf16[256,768]{1,0:T(8,128)(2,1)}, bf16[256,768]{1,0:T(8,128)(2,1)S(1)}, u32[]{:S(2)}) copy-start(bf16[256,768]{1,0:T(8,128)(2,1)S(1)} %collective-permute-done.1) | copy-start | bytes 1179652
  70.6 24.0 %copy-start.8 = (f32[256,256]{0,1:T(8,128)}, f32[256,256]{0,1:T(8,128)S(1)}, u32[]{:S(2)}) copy-start(f32[256,256]{0,1:T(8,128)S(1)} %get-tuple-element.9) | copy-start | bytes 786436
  70.9 23.7 %collective-permute-start.8 = (f32[256,768]{1,0:T(8,128)S(1)}, f32[256,768]{1,0:T(8,128)S(1)}, u32[]{:S(2)}, u32[]{:S(2)}) collective-permute-start(f32[256,768]{1,0:T(8,128)S(1)} %fusion.56), channel_id=1, source_target_pairs={{0,4},{4,8},{8,12},{12,16},{16,20},{20,24},{24,28},{28,32},{32,36}... | collective-permute-start | bytes 2359304 | tf_op jit(solution)/shard_map/ppermute | solution.py:11
  75.5 12.5 %collective-permute-start.3 = (bf16[256,768]{1,0:T(8,128)(2,1)S(1)}, bf16[256,768]{1,0:T(8,128)(2,1)}, u32[]{:S(2)}, u32[]{:S(2)}) collective-permute-start(bf16[256,768]{1,0:T(8,128)(2,1)S(1)} %collective-permute-done.1), channel_id=1, source_target_pairs={{0,4},{4,8},{8,12},{12,16},{16,20},{20,24},{24,28},{28,32},{32,36}... | collective-permute-start | bytes 1179656 | tf_op jit(solution)/shard_map/ppermute | solution.py:11
  79.3 17.9 %copy-start.5 = (f32[256,256]{1,0:T(8,128)}, f32[256,256]{1,0:T(8,128)S(1)}, u32[]{:S(2)}) copy-start(f32[256,256]{1,0:T(8,128)S(1)} %get-tuple-element.7) | copy-start | bytes 786436
  79.3 17.9 %copy-start.7 = (pred[256,256]{0,1:T(32,128)(4,1)S(1)}, pred[256,256]{0,1:T(32,128)(4,1)}, u32[]{:S(2)}) copy-start(pred[256,256]{0,1:T(32,128)(4,1)} %get-tuple-element.4) | copy-start | bytes 196612
  87.9 35.4 %collective-permute-start.5 = (bf16[256,768]{1,0:T(8,128)(2,1)}, bf16[256,768]{1,0:T(8,128)(2,1)}, u32[]{:S(2)}, u32[]{:S(2)}) collective-permute-start(bf16[256,768]{1,0:T(8,128)(2,1)} %collective-permute-done.3), channel_id=1, source_target_pairs={{0,4},{4,8},{8,12},{12,16},{16,20},{20,24},{24,28},{28,32},{32,36}... | collective-permute-start | bytes 1179656 | tf_op jit(solution)/shard_map/ppermute | solution.py:11
  94.9 56.4 %collective-permute-start.9 = (f32[256,768]{1,0:T(8,128)S(1)}, f32[256,768]{1,0:T(8,128)S(1)}, u32[]{:S(2)}, u32[]{:S(2)}) collective-permute-start(f32[256,768]{1,0:T(8,128)S(1)} %convolution_add_fusion), channel_id=1, source_target_pairs={{0,4},{4,8},{8,12},{12,16},{16,20},{20,24},{24,28},{28,32},{32,36}... | collective-permute-start | bytes 2359304 | tf_op jit(solution)/shard_map/ppermute | solution.py:11
  123.3 36.3 %collective-permute-start.7 = (bf16[256,768]{1,0:T(8,128)(2,1)}, bf16[256,768]{1,0:T(8,128)(2,1)S(1)}, u32[]{:S(2)}, u32[]{:S(2)}) collective-permute-start(bf16[256,768]{1,0:T(8,128)(2,1)} %collective-permute-done.5), channel_id=1, source_target_pairs={{0,4},{4,8},{8,12},{12,16},{16,20},{20,24},{24,28},{28,32},{32,36}... | collective-permute-start | bytes 1179656 | tf_op jit(solution)/shard_map/ppermute | solution.py:11
  152.5 124.0 %collective-permute-start.10 = (f32[256,768]{1,0:T(8,128)}, f32[256,768]{1,0:T(8,128)}, u32[]{:S(2)}, u32[]{:S(2)}) collective-permute-start(f32[256,768]{1,0:T(8,128)} %fusion.51), channel_id=1, source_target_pairs={{0,4},{4,8},{8,12},{12,16},{16,20},{20,24},{24,28},{28,32},{32,36}... | collective-permute-start | bytes 2359304 | tf_op jit(solution)/shard_map/ppermute | solution.py:11
  276.5 7.8 %copy-start.11 = (pred[4]{0:T(512)(128)(4,1)S(1)}, pred[4]{0:T(512)(128)(4,1)}, u32[]{:S(2)}) copy-start(pred[4]{0:T(512)(128)(4,1)} %fusion.33) | copy-start | bytes 16
  278.0 20.9 %collective-permute-start.11 = (f32[256,768]{1,0:T(8,128)S(1)}, f32[256,768]{1,0:T(8,128)S(1)}, u32[]{:S(2)}, u32[]{:S(2)}) collective-permute-start(f32[256,768]{1,0:T(8,128)S(1)} %fusion.45), channel_id=1, source_target_pairs={{0,752},{4,756},{8,760},{12,764},{16,0},{20,4},{24,8},{28,12},{32,... | collective-permute-start | bytes 2359304 | tf_op jit(solution)/shard_map/ppermute | solution.py:11
  284.3 14.6 %copy-start.6 = (f32[256,256]{1,0:T(8,128)S(1)}, f32[256,256]{1,0:T(8,128)}, u32[]{:S(2)}) copy-start(f32[256,256]{1,0:T(8,128)} %copy-done.5) | copy-start | bytes 786436
Sparse Core Ops, SparseCore 0:
  10.4 54.7 all-gather.3
  69.6 84.7 all-gather.5
where the time goes:
time: 310 us; the launch traced here: 308 us
  blocking collectives  123 us (40%)
  waiting for transfers between devices  96 us (31%)
  starting transfers between devices  37.1 us (12%)
  between operations  21.4 us (7%)
  matrix products  20.7 us (7%)
  other arithmetic  7.82 us (3%)
    psum x1, blocking collectives, body(): loss = lax.psum(loss_total, ('blk', 'group')) / jnp.float32(pair_count)  112 us
    ppermute x12, waiting for transfers between devices, shifted(): lax.ppermute(array, axis, [(i, (i + by) % count) for i in range(count)])  85.7 us
    ppermute x12, starting transfers between devices, shifted(): lax.ppermute(array, axis, [(i, (i + by) % count) for i in range(count)])  37 us
    all_gather x1, blocking collectives, body(): piece_ids = lax.all_gather(caption_ids, 'group', axis=0, tiled=True)  10.3 us
    all_gather x1, waiting for transfers between devices, body(): piece_text = lax.all_gather(text_embed, 'group', axis=0, tiled=True)  9.53 us
    dot_general x6, matrix products, block_terms(): lax.dot_general(audio, text, (((1,), (1,)), ((), ())), preferred_element_...  7.96 us
    dot_general x6, matrix products, block_terms(): grad_a = jnp.dot(coeff, text, preferred_element_type=jnp.float32)  7.01 us
  transfers between devices with their start and end apart: 14, of which 8 were waited for; matrix products, arithmetic and copies ran while one was open for 10% of the time, Pallas kernels for 0%

commit v1 on v0

v1 whole, which is shorter than its diff:
```python
import functools
import itertools

import jax
import jax.numpy as jnp
import numpy as np
from jax import lax
from jax.experimental import pallas as pl
from jax.experimental.pallas import tpu as pltpu
from jax.sharding import PartitionSpec as P

SPLIT = 64
MARKS = 16
AXES = ("z", "x", "yl", "core", "group")
BLK = AXES[:4]
PERMS = list(itertools.permutations(range(4)))


def shifted(array, by):
    count = lax.axis_size(BLK)
    return lax.ppermute(array, BLK, [(i, (i + by) % count) for i in range(count)])


def core_swap(array):
    return lax.ppermute(array, "core", [(0, 1), (1, 0)])


def after(array, *earlier):
    return lax.optimization_barrier((array,) + earlier)[0]


def pair_margin(scale, bias, ids, mine, other):
    rows = ids.shape[0]
    dots = lax.dot_general(
        mine, other[:rows, :], (((1,), (1,)), ((), ())), preferred_element_type=jnp.float32
    )
    marks = other[rows:, :rows].astype(jnp.float32)
    same = ids == marks[0:1] * SPLIT + marks[1:2]
    logits = scale * dots + bias
    return same, jnp.where(same, logits, -logits)


def start_loads(sources, targets, sems):
    for i, (source, target) in enumerate(zip(sources, targets)):
        pltpu.make_async_copy(source, target, sems.at[i]).start()


def wait_load(source, target, sems, i):
    pltpu.make_async_copy(source, target, sems.at[i]).wait()


def loss_kernel(n_text, count, scalars, own_ids, audio, text, *refs):
    others = refs[:count]
    out, own, held, sems = refs[count:]
    start_loads(
        (audio, text) + others, [own.at[0], own.at[1]] + [held.at[i] for i in range(count)], sems
    )
    wait_load(audio, own.at[0], sems, 0)
    wait_load(text, own.at[1], sems, 1)
    rows = own_ids.shape[0]
    total = jnp.zeros((1, rows), jnp.float32)
    for i in range(-1, count):
        kind = 1 if i >= n_text else 0
        other = own.at[1] if i < 0 else held.at[i]
        if i >= 0:
            wait_load(text, held.at[i], sems, i + 2)
        _, margin = pair_margin(scalars[0], scalars[1], own_ids[...], own[kind, :rows, :], other)
        tail = jnp.log1p(jnp.exp(-jnp.abs(margin)))
        total += jnp.sum(jnp.maximum(-margin, 0.0) + tail, axis=0, keepdims=True)
    out[...] = total[:, :128] + total[:, 128:]


def grad_kernel(n_text, count, scalars, own_ids, audio, text, *refs):
    others = refs[:count]
    grad_audio, grad_text, own, held, sems = refs[count:]
    rows = own_ids.shape[0]
    start_loads(
        (audio, text) + others, [own.at[0], own.at[1]] + [held.at[i] for i in range(count)], sems
    )
    wait_load(audio, own.at[0], sems, 0)
    wait_load(text, own.at[1], sems, 1)

    def term(mine, other):
        scale = scalars[0]
        same, margin = pair_margin(scale, scalars[1], own_ids[...], mine[:rows, :], other)
        tail = jnp.exp(-jnp.abs(margin))
        weight = jnp.where(margin >= 0.0, tail, 1.0) / (1.0 + tail)
        coeff = (jnp.where(same, -scale, scale) * weight).astype(jnp.bfloat16)
        return jnp.dot(coeff, other[:rows, :], preferred_element_type=jnp.float32)

    for kind, (grad, indices) in enumerate(
        ((grad_audio, range(n_text)), (grad_text, range(n_text, count)))
    ):
        acc = term(own.at[kind], own.at[1 - kind])
        for i in indices:
            wait_load(text, held.at[i], sems, i + 2)
            acc += term(own.at[kind], held.at[i])
        grad[...] = acc.astype(jnp.bfloat16)


def call(kernel, scalars, own_ids, audio, text, texts, audios, out_shape, flops):
    blocks = tuple(texts) + tuple(audios)
    count = len(blocks)
    whole = pl.BlockSpec(memory_space=pltpu.VMEM)
    anywhere = pl.BlockSpec(memory_space=pl.ANY)
    return pl.pallas_call(
        functools.partial(kernel, len(texts), count),
        out_shape=out_shape,
        in_specs=[pl.BlockSpec(memory_space=pltpu.SMEM), whole] + [anywhere] * (2 + count),
        out_specs=jax.tree.map(lambda _: whole, out_shape),
        scratch_shapes=[
            pltpu.VMEM((2,) + text.shape, text.dtype),
            pltpu.VMEM((count,) + text.shape, text.dtype),
            pltpu.SemaphoreType.DMA((2 + count,)),
        ],
        compiler_params=pltpu.CompilerParams(vmem_limit_bytes=24 * 1024 * 1024),
        cost_estimate=pl.CostEstimate(
            flops=flops, bytes_accessed=2 * (count + 2) * text.size, transcendentals=0
        ),
    )(scalars, own_ids, audio, text, *blocks)


def losses(scalars, own_ids, audio, text, texts, audios):
    rows = own_ids.shape[0]
    return call(
        loss_kernel,
        scalars,
        own_ids,
        audio,
        text,
        texts,
        audios,
        jax.ShapeDtypeStruct((1, 128), jnp.float32),
        2 * (1 + len(texts) + len(audios)) * rows * text.size,
    )


def gradients(scalars, own_ids, audio, text, texts, audios):
    rows = own_ids.shape[0]
    shape = (rows, text.shape[1])
    return call(
        grad_kernel,
        scalars,
        own_ids,
        audio,
        text,
        texts,
        audios,
        [jax.ShapeDtypeStruct(shape, jnp.bfloat16)] * 2,
        4 * (2 + len(texts) + len(audios)) * rows * text.size,
    )


def spread_sum(row, axes):
    count = lax.axis_size(axes)
    copies = jnp.broadcast_to(row[None], (count,) + row.shape)
    return jnp.sum(lax.all_to_all(copies, axes, 0, 0, tiled=True), axis=0)


def exchange(perm, text, audio):
    first = lax.axis_index("core") == 0
    forward = [(p, g) for g, p in enumerate(perm)]
    backward = [(g, p) for g, p in enumerate(perm)]
    partner_text, partner_audio = text, audio
    moved = forward != [(g, g) for g in range(len(perm))]
    text4 = shifted(text, 4)
    audio2 = shifted(audio, -2)
    if moved:
        partner_text = lax.ppermute(text, "group", forward)
    text2 = shifted(text, 2)
    audio4 = shifted(audio, -4)
    if moved:
        source = after(audio, partner_text) if set(forward) == set(backward) else audio
        partner_audio = lax.ppermute(source, "group", backward)
    text_x = core_swap(jnp.where(first, text, text4))
    audio_x = core_swap(audio2)
    text_y = core_swap(text2)
    audio_y = core_swap(jnp.where(first, audio4, audio))
    return (
        (text4, text_x, partner_text, text2, text_y),
        (audio2, audio_x, audio4, audio_y, partner_audio),
    )


def body(audio_embed, text_embed, caption_ids, pairing, logit_scale, logit_bias):
    rows, width = audio_embed.shape
    pair_count = rows * lax.axis_size(AXES)
    scalars = jnp.concatenate([logit_scale, logit_bias])
    high = (caption_ids // SPLIT).astype(jnp.bfloat16)
    low = (caption_ids % SPLIT).astype(jnp.bfloat16)
    marks = jnp.pad(jnp.stack([high, low]), ((0, MARKS - 2), (0, width - rows)))
    text = jnp.concatenate([text_embed, marks])
    audio = jnp.concatenate([audio_embed, marks])
    own_ids = caption_ids.astype(jnp.float32).reshape(rows, 1)
    index = jnp.argmax(jnp.all(jnp.asarray(np.array(PERMS, np.int32)) == pairing[None], axis=1))
    texts, audios = lax.switch(
        index, [functools.partial(exchange, perm) for perm in PERMS], text, audio
    )
    terms = losses(scalars, own_ids, audio, text, texts[:3], audios[:2])
    total = spread_sum(spread_sum(terms, ("yl", "core", "group")), ("z", "x"))
    grad_audio, grad_text = gradients(scalars, own_ids, audio, text, texts, audios)
    return jnp.sum(total) / jnp.float32(pair_count), grad_audio, grad_text


def solution(mesh):
    inner = jax.sharding.Mesh(mesh.devices.reshape(12, 4, 2, 2, 4), AXES)
    placed = (P(AXES, None), P(AXES, None), P(AXES), P(), P(), P())
    return jax.shard_map(
        body,
        mesh=inner,
        in_specs=placed,
        out_specs=(P(), P(AXES, None), P(AXES, None)),
        check_vma=False,
    )
```

time: 310 us -> 109 us (0.35)
  blocking collectives: 123 us -> 10.6 us
  waiting for transfers between devices: 96 us -> 16 us
  matrix products: 20.7 us -> 0 us
  starting transfers between devices: 37.1 us -> 56.9 us
  between operations: 21.4 us -> 4.45 us
  Pallas kernels: 0 us -> 13.7 us
  other arithmetic: 7.82 us -> 4.5 us
    psum x1 -> x0, blocking collectives: 112 us -> none  [body(): loss = lax.psum(loss_total, ('blk', 'group')) / jnp.float32(pair_count)]
    ppermute x12 -> x10, waiting for transfers between devices: 85.7 us -> 14.1 us  [the longest x4 6.56 us: shifted(): lax.ppermute(array, BLK, [(i, (i + by) % count) for i in range(count)])]
    dot_general x18 -> x0, matrix products: 20.7 us -> none  [the longest x6 7.96 us: block_terms(): lax.dot_general(audio, text, (((1,), (1,)), ((), ())), preferred_element_...]
    pallas_call x0 -> x2, Pallas kernels: none -> 13.7 us  [call(): pl.pallas_call(functools.partial(kernel, len(texts), count), out_shape=ou...]
    ppermute x12 -> x10, starting transfers between devices: 37 us -> 48.7 us  [the longest x4 28.8 us: shifted(): lax.ppermute(array, BLK, [(i, (i + by) % count) for i in range(count)])]
    all_to_all x0 -> x1, blocking collectives: none -> 10.6 us  [spread_sum(): return jnp.sum(lax.all_to_all(copies, axes, 0, 0, tiled=True), axis=0)]
    all_gather x1 -> x0, blocking collectives: 10.3 us -> none  [body(): piece_ids = lax.all_gather(caption_ids, 'group', axis=0, tiled=True)]
    all_gather x2 -> x0, waiting for transfers between devices: 9.53 us -> none  [the longest x1 9.53 us: body(): piece_text = lax.all_gather(text_embed, 'group', axis=0, tiled=True)]
  transfers between devices with their start and end apart: 14 -> 11, of which waited for: 8 -> 5; matrix products, arithmetic and copies ran while one was open for 10% -> 1% of each run, Pallas kernels for 0% -> 8%
where the time goes in v1:
time: 109 us; the launch traced here: 108 us
  starting transfers between devices  56.9 us (52%)
  waiting for transfers between devices  16 us (15%)
  Pallas kernels  13.7 us (13%)
  blocking collectives  10.6 us (10%)
  other arithmetic  4.5 us (4%)
  between operations  4.45 us (4%)
  local copies, waits for them, and re-layouts  1.44 us (1%)
    ppermute x4, starting transfers between devices, shifted(): lax.ppermute(array, BLK, [(i, (i + by) % count) for i in range(count)])  28.8 us
    pallas_call x2, Pallas kernels, call(): pl.pallas_call(functools.partial(kernel, len(texts), count), out_shape=ou...  13.7 us
    ppermute x4, starting transfers between devices, core_swap(): return lax.ppermute(array, 'core', [(0, 1), (1, 0)])  12.2 us
    all_to_all x1, blocking collectives, spread_sum(): return jnp.sum(lax.all_to_all(copies, axes, 0, 0, tiled=True), axis=0)  10.6 us
    all_to_all x1, starting transfers between devices, spread_sum(): return jnp.sum(lax.all_to_all(copies, axes, 0, 0, tiled=True), axis=0)  8.12 us
    ppermute x4, waiting for transfers between devices, shifted(): lax.ppermute(array, BLK, [(i, (i + by) % count) for i in range(count)])  6.56 us
    ppermute x1, waiting for transfers between devices, exchange(): partner_text = lax.ppermute(text, 'group', forward)  5.89 us
    ppermute x1, starting transfers between devices, exchange(): partner_text = lax.ppermute(text, 'group', forward)  4.22 us
  transfers between devices with their start and end apart: 11, of which 5 were waited for; matrix products, arithmetic and copies ran while one was open for 1% of the time, Pallas kernels for 8%

profile of v1, /device:TPU:1, one launch (start us, length us, event | category | flops | bytes accessed | tf_op | source)
XLA Modules:
  0.0 107.9 jit_solution(11524701573352878073)
XLA Ops:
  0.6 0.8 fusion.7
  1.4 0.0 copy-start
  1.4 0.0 copy-start.1
  1.4 0.6 copy-done
  2.1 0.0 copy-done.1
  2.1 0.1 compare_reduce_fusion
  2.2 0.7 iota_reduce_fusion
  2.8 0.1 copy.14.own_ids
  4.3 1.2 %pad_maximum_fusion = (bf16[272,768]{1,0:T(8,128)(2,1)S(1)}, bf16[272,768]{1,0:T(8,128)(2,1)S(1)}) fusion(bf16[16,768]{1,0:T(8,128)(2,1)S(1)} %fusion.5, bf16[256,768]{1,0:T(8,128)(2,1)} %param.32, bf16[256,768]{1,0:T(8,128)(2,1)} %param.31), kind=kLoop, calls=%fused_computation.48 | loop fusion | flops 1462272 | bytes 1646592 | tf_op jit(solution)/shard_map/concatenate | solution.py:192
  6.1 64.3 %conditional.1 = (bf16[272,768]{1,0:T(8,128)(2,1)}, bf16[272,768]{1,0:T(8,128)(2,1)}, bf16[272,768]{1,0:T(8,128)(2,1)}, bf16[272,768]{1,0:T(8,128)(2,1)}, bf16[2...) conditional(s32[]{:T(128)} %clamp.3, ...), branch_computations={%region_2.3_spmd, %region_3.4_spmd, %region_4.5_spmd, %region_5.6_... | conditional | flops 417796 | bytes 19218956 | solution.py:196
  6.3 4.0 %collective-permute-start.178 = (bf16[272,768]{1,0:T(8,128)(2,1)S(1)}, bf16[272,768]{1,0:T(8,128)(2,1)}, u32[]{:S(2)}, u32[]{:S(2)}) collective-permute-start(bf16[272,768]{1,0:T(8,128)(2,1)S(1)} %get-tuple-element.139), channel_id=1, source_target_pairs={{0,16},{4,20},{8,24},{12,28},{16,32},{20,36},{24,40},{28,44},{32,4... | collective-permute-start | bytes 1253384 | tf_op jit(solution)/shard_map/cond/branch_18_fun/ppermute | solution.py:21
  10.3 15.3 %collective-permute-start.185 = (bf16[272,768]{1,0:T(8,128)(2,1)S(1)}, bf16[272,768]{1,0:T(8,128)(2,1)}, u32[]{:S(2)}, u32[]{:S(2)}) collective-permute-start(bf16[272,768]{1,0:T(8,128)(2,1)S(1)} %get-tuple-element.140), channel_id=1, source_target_pairs={{0,752},{4,756},{8,760},{12,764},{16,0},{20,4},{24,8},{28,12},{32,... | collective-permute-start | bytes 1253384 | tf_op jit(solution)/shard_map/cond/branch_18_fun/ppermute | solution.py:21
  25.6 3.2 %collective-permute-start.181 = (bf16[272,768]{1,0:T(8,128)(2,1)S(1)}, bf16[272,768]{1,0:T(8,128)(2,1)}, u32[]{:S(2)}, u32[]{:S(2)}) collective-permute-start(bf16[272,768]{1,0:T(8,128)(2,1)S(1)} %get-tuple-element.139), channel_id=1, source_target_pairs={{0,8},{4,12},{8,16},{12,20},{16,24},{20,28},{24,32},{28,36},{32,40... | collective-permute-start | bytes 1253384 | tf_op jit(solution)/shard_map/cond/branch_18_fun/ppermute | solution.py:21
  28.8 6.3 %collective-permute-start.183 = (bf16[272,768]{1,0:T(8,128)(2,1)S(1)}, bf16[272,768]{1,0:T(8,128)(2,1)}, u32[]{:S(2)}, u32[]{:S(2)}) collective-permute-start(bf16[272,768]{1,0:T(8,128)(2,1)S(1)} %get-tuple-element.140), channel_id=1, source_target_pairs={{0,760},{4,764},{8,0},{12,4},{16,8},{20,12},{24,16},{28,20},{32,24... | collective-permute-start | bytes 1253384 | tf_op jit(solution)/shard_map/cond/branch_18_fun/ppermute | solution.py:21
  35.1 4.2 %collective-permute-start.180 = (bf16[272,768]{1,0:T(8,128)(2,1)S(1)}, bf16[272,768]{1,0:T(8,128)(2,1)}, u32[]{:S(2)}, u32[]{:S(2)}) collective-permute-start(bf16[272,768]{1,0:T(8,128)(2,1)S(1)} %get-tuple-element.139), channel_id=1, source_target_pairs={{3,0},{0,1},{1,2},{2,3},{7,4},{4,5},{5,6},{6,7},{11,8},{8,9},{9,10... | collective-permute-start | bytes 1253384 | tf_op jit(solution)/shard_map/cond/branch_18_fun/ppermute | solution.py:169
  39.4 0.0 collective-permute-done.178
  39.4 3.6 %collective-permute-start.187 = (bf16[272,768]{1,0:T(8,128)(2,1)S(1)}, bf16[272,768]{1,0:T(8,128)(2,1)}, u32[]{:S(2)}, u32[]{:S(2)}) collective-permute-start(bf16[272,768]{1,0:T(8,128)(2,1)S(1)} %get-tuple-element.140), channel_id=1, source_target_pairs={{0,3},{1,0},{2,1},{3,2},{4,7},{5,4},{6,5},{7,6},{8,11},{9,8},{10,9... | collective-permute-start | bytes 1253384 | tf_op jit(solution)/shard_map/cond/branch_18_fun/ppermute | solution.py:174
  43.0 1.1 broadcast_select_fusion.37
  44.0 0.0 collective-permute-done.185
  44.0 2.7 %collective-permute-start.179 = (bf16[272,768]{1,0:T(8,128)(2,1)S(1)}, bf16[272,768]{1,0:T(8,128)(2,1)}, u32[]{:S(2)}, u32[]{:S(2)}) collective-permute-start(bf16[272,768]{1,0:T(8,128)(2,1)S(1)} %broadcast_select_fusion.37), channel_id=1, source_target_pairs={{0,4},{4,0},{1,5},{5,1},{2,6},{6,2},{3,7},{7,3},{8,12},{12,8},{9,1... | collective-permute-start | bytes 1253384 | tf_op jit(solution)/shard_map/cond/branch_18_fun/ppermute | solution.py:25
  46.8 0.1 broadcast_select_fusion.36
  46.8 5.8 %collective-permute-done.181 = bf16[272,768]{1,0:T(8,128)(2,1)} collective-permute-done((bf16[272,768]{1,0:T(8,128)(2,1)S(1)}, bf16[272,768]{1,0:T(8,128)(2,1)}, u32[]{:S(2)}, u32[]{:S(2)}) %collective-permute-start.181) | collective-permute-done | bytes 417824 | tf_op jit(solution)/shard_map/cond/branch_18_fun/ppermute | solution.py:21
  52.7 2.5 %collective-permute-start.186 = (bf16[272,768]{1,0:T(8,128)(2,1)S(1)}, bf16[272,768]{1,0:T(8,128)(2,1)}, u32[]{:S(2)}, u32[]{:S(2)}) collective-permute-start(bf16[272,768]{1,0:T(8,128)(2,1)S(1)} %broadcast_select_fusion.36), channel_id=1, source_target_pairs={{0,4},{4,0},{1,5},{5,1},{2,6},{6,2},{3,7},{7,3},{8,12},{12,8},{9,1... | collective-permute-start | bytes 1253384 | tf_op jit(solution)/shard_map/cond/branch_18_fun/ppermute | solution.py:25
  55.1 0.7 collective-permute-done.183
  55.9 4.6 %collective-permute-start.182 = (bf16[272,768]{1,0:T(8,128)(2,1)}, bf16[272,768]{1,0:T(8,128)(2,1)}, u32[]{:S(2)}, u32[]{:S(2)}) collective-permute-start(bf16[272,768]{1,0:T(8,128)(2,1)} %collective-permute-done.181), channel_id=1, source_target_pairs={{0,4},{4,0},{1,5},{5,1},{2,6},{6,2},{3,7},{7,3},{8,12},{12,8},{9,1... | collective-permute-start | bytes 1253384 | tf_op jit(solution)/shard_map/cond/branch_18_fun/ppermute | solution.py:25
  60.5 5.9 %collective-permute-done.180 = bf16[272,768]{1,0:T(8,128)(2,1)} collective-permute-done((bf16[272,768]{1,0:T(8,128)(2,1)S(1)}, bf16[272,768]{1,0:T(8,128)(2,1)}, u32[]{:S(2)}, u32[]{:S(2)}) %collective-permute-start.180) | collective-permute-done | bytes 417824 | tf_op jit(solution)/shard_map/cond/branch_18_fun/ppermute | solution.py:169
  66.4 2.4 %collective-permute-start.184 = (bf16[272,768]{1,0:T(8,128)(2,1)}, bf16[272,768]{1,0:T(8,128)(2,1)}, u32[]{:S(2)}, u32[]{:S(2)}) collective-permute-start(bf16[272,768]{1,0:T(8,128)(2,1)} %collective-permute-done.183), channel_id=1, source_target_pairs={{0,4},{4,0},{1,5},{5,1},{2,6},{6,2},{3,7},{7,3},{8,12},{12,8},{9,1... | collective-permute-start | bytes 1253384 | tf_op jit(solution)/shard_map/cond/branch_18_fun/ppermute | solution.py:25
  68.8 0.0 collective-permute-done.187
  68.8 0.0 collective-permute-done.179
  68.8 0.0 collective-permute-done.186
  68.8 0.0 collective-permute-done.182
  68.8 1.7 %collective-permute-done.184 = bf16[272,768]{1,0:T(8,128)(2,1)} collective-permute-done((bf16[272,768]{1,0:T(8,128)(2,1)}, bf16[272,768]{1,0:T(8,128)(2,1)}, u32[]{:S(2)}, u32[]{:S(2)}) %collective-permute-start.184) | collective-permute-done | bytes 417824 | tf_op jit(solution)/shard_map/cond/branch_18_fun/ppermute | solution.py:25
  70.5 0.1 pad_maximum_fusion.2.scalars
  70.5 4.7 %shard_map.94 = f32[1,128]{1,0:T(1,128)S(1)} custom-call(f32[2]{0:T(128)S(1)} %pad_maximum_fusion.2.scalars, f32[256,1]{1,0:T(8,128)S(1)} %copy.14.own_ids, bf16[272,768]{1,0:T(8,128)(2,1)S(1)} %get-tuple-element.183.audio, bf16[272,768]{1,0:T(8,128)(2,1)S(1)} %get-tuple-element.182.text, bf16[272,768]{1,0:T(8,128)(2,1)} %get-tuple-element.170.refs_0_, ...), custom_call_target="tpu_custom_call" | custom-call | flops 641728512 | bytes 2924544 | tf_op jit(solution)/shard_map/pallas_call | solution.py:106
  75.2 10.6 %all_to_all.10 = f32[16,1,128]{2,1,0:T(1,128)S(1)} all-to-all(f32[16,1,128]{2,1,0:T(1,128)S(1)} %broadcast_in_dim.7), channel_id=1, replica_groups=mesh['z'=12,'x'=4,'yl'=2,'core'=2,'group'=4] {'yl','core','group'}, dimensions={0} | all-to-all | bytes 16384 | tf_op jit(solution)/shard_map/all_to_all | solution.py:157
  85.8 0.6 broadcast_in_dim.8
  86.5 8.1 %all-to-all-start.1 = ((f32[48,1,128]{2,1,0:T(1,128)}), f32[48,1,128]{2,1,0:T(1,128)S(1)}, u32[]{:S(2)}, u32[]{:S(2)}) async-start(f32[48,1,128]{2,1,0:T(1,128)} %broadcast_in_dim.8), calls=%async_computation.1 | async-start | bytes 49152 | tf_op jit(solution)/shard_map/all_to_all | solution.py:157
  94.6 9.1 %shard_map.95 = (bf16[256,768]{1,0:T(8,128)(2,1)}, bf16[256,768]{1,0:T(8,128)(2,1)}) custom-call(f32[2]{0:T(128)S(1)} %pad_maximum_fusion.2.scalars, f32[256,1]{1,0:T(8,128)S(1)} %copy.14.own_ids, bf16[272,768]{1,0:T(8,128)(2,1)S(1)} %get-tuple-element.183.audio, bf16[272,768]{1,0:T(8,128)(2,1)S(1)} %get-tuple-element.182.text, ...), custom_call_target="tpu_custom_call" | custom-call | flops 2566914048 | bytes 5013504 | tf_op jit(solution)/shard_map/pallas_call | solution.py:106
  103.7 1.9 %all-to-all-done.1 = f32[48,1,128]{2,1,0:T(1,128)S(1)} async-done(((f32[48,1,128]{2,1,0:T(1,128)}), f32[48,1,128]{2,1,0:T(1,128)S(1)}, u32[]{:S(2)}, u32[]{:S(2)}) %all-to-all-start.1) | async-done | bytes 24608 | tf_op jit(solution)/shard_map/all_to_all | solution.py:157
  105.5 0.6 reduce_sum.20
  (5 shorter events, 0.0 us)
Async XLA Ops:
  1.4 0.7 copy-start
  1.4 0.7 copy-start.1
  6.3 33.0 %collective-permute-start.178 = (bf16[272,768]{1,0:T(8,128)(2,1)S(1)}, bf16[272,768]{1,0:T(8,128)(2,1)}, u32[]{:S(2)}, u32[]{:S(2)}) collective-permute-start(bf16[272,768]{1,0:T(8,128)(2,1)S(1)} %get-tuple-element.139), channel_id=1, source_target_pairs={{0,16},{4,20},{8,24},{12,28},{16,32},{20,36},{24,40},{28,44},{32,4... | collective-permute-start | bytes 1253384 | tf_op jit(solution)/shard_map/cond/branch_18_fun/ppermute | solution.py:21
  10.3 33.7 %collective-permute-start.185 = (bf16[272,768]{1,0:T(8,128)(2,1)S(1)}, bf16[272,768]{1,0:T(8,128)(2,1)}, u32[]{:S(2)}, u32[]{:S(2)}) collective-permute-start(bf16[272,768]{1,0:T(8,128)(2,1)S(1)} %get-tuple-element.140), channel_id=1, source_target_pairs={{0,752},{4,756},{8,760},{12,764},{16,0},{20,4},{24,8},{28,12},{32,... | collective-permute-start | bytes 1253384 | tf_op jit(solution)/shard_map/cond/branch_18_fun/ppermute | solution.py:21
  25.6 27.0 %collective-permute-start.181 = (bf16[272,768]{1,0:T(8,128)(2,1)S(1)}, bf16[272,768]{1,0:T(8,128)(2,1)}, u32[]{:S(2)}, u32[]{:S(2)}) collective-permute-start(bf16[272,768]{1,0:T(8,128)(2,1)S(1)} %get-tuple-element.139), channel_id=1, source_target_pairs={{0,8},{4,12},{8,16},{12,20},{16,24},{20,28},{24,32},{28,36},{32,40... | collective-permute-start | bytes 1253384 | tf_op jit(solution)/shard_map/cond/branch_18_fun/ppermute | solution.py:21
  28.8 27.0 %collective-permute-start.183 = (bf16[272,768]{1,0:T(8,128)(2,1)S(1)}, bf16[272,768]{1,0:T(8,128)(2,1)}, u32[]{:S(2)}, u32[]{:S(2)}) collective-permute-start(bf16[272,768]{1,0:T(8,128)(2,1)S(1)} %get-tuple-element.140), channel_id=1, source_target_pairs={{0,760},{4,764},{8,0},{12,4},{16,8},{20,12},{24,16},{28,20},{32,24... | collective-permute-start | bytes 1253384 | tf_op jit(solution)/shard_map/cond/branch_18_fun/ppermute | solution.py:21
  35.1 31.2 %collective-permute-start.180 = (bf16[272,768]{1,0:T(8,128)(2,1)S(1)}, bf16[272,768]{1,0:T(8,128)(2,1)}, u32[]{:S(2)}, u32[]{:S(2)}) collective-permute-start(bf16[272,768]{1,0:T(8,128)(2,1)S(1)} %get-tuple-element.139), channel_id=1, source_target_pairs={{3,0},{0,1},{1,2},{2,3},{7,4},{4,5},{5,6},{6,7},{11,8},{8,9},{9,10... | collective-permute-start | bytes 1253384 | tf_op jit(solution)/shard_map/cond/branch_18_fun/ppermute | solution.py:169
  39.4 29.4 %collective-permute-start.187 = (bf16[272,768]{1,0:T(8,128)(2,1)S(1)}, bf16[272,768]{1,0:T(8,128)(2,1)}, u32[]{:S(2)}, u32[]{:S(2)}) collective-permute-start(bf16[272,768]{1,0:T(8,128)(2,1)S(1)} %get-tuple-element.140), channel_id=1, source_target_pairs={{0,3},{1,0},{2,1},{3,2},{4,7},{5,4},{6,5},{7,6},{8,11},{9,8},{10,9... | collective-permute-start | bytes 1253384 | tf_op jit(solution)/shard_map/cond/branch_18_fun/ppermute | solution.py:174
  44.0 24.7 %collective-permute-start.179 = (bf16[272,768]{1,0:T(8,128)(2,1)S(1)}, bf16[272,768]{1,0:T(8,128)(2,1)}, u32[]{:S(2)}, u32[]{:S(2)}) collective-permute-start(bf16[272,768]{1,0:T(8,128)(2,1)S(1)} %broadcast_select_fusion.37), channel_id=1, source_target_pairs={{0,4},{4,0},{1,5},{5,1},{2,6},{6,2},{3,7},{7,3},{8,12},{12,8},{9,1... | collective-permute-start | bytes 1253384 | tf_op jit(solution)/shard_map/cond/branch_18_fun/ppermute | solution.py:25
  52.7 16.1 %collective-permute-start.186 = (bf16[272,768]{1,0:T(8,128)(2,1)S(1)}, bf16[272,768]{1,0:T(8,128)(2,1)}, u32[]{:S(2)}, u32[]{:S(2)}) collective-permute-start(bf16[272,768]{1,0:T(8,128)(2,1)S(1)} %broadcast_select_fusion.36), channel_id=1, source_target_pairs={{0,4},{4,0},{1,5},{5,1},{2,6},{6,2},{3,7},{7,3},{8,12},{12,8},{9,1... | collective-permute-start | bytes 1253384 | tf_op jit(solution)/shard_map/cond/branch_18_fun/ppermute | solution.py:25
  55.9 12.9 %collective-permute-start.182 = (bf16[272,768]{1,0:T(8,128)(2,1)}, bf16[272,768]{1,0:T(8,128)(2,1)}, u32[]{:S(2)}, u32[]{:S(2)}) collective-permute-start(bf16[272,768]{1,0:T(8,128)(2,1)} %collective-permute-done.181), channel_id=1, source_target_pairs={{0,4},{4,0},{1,5},{5,1},{2,6},{6,2},{3,7},{7,3},{8,12},{12,8},{9,1... | collective-permute-start | bytes 1253384 | tf_op jit(solution)/shard_map/cond/branch_18_fun/ppermute | solution.py:25
  66.4 4.1 %collective-permute-start.184 = (bf16[272,768]{1,0:T(8,128)(2,1)}, bf16[272,768]{1,0:T(8,128)(2,1)}, u32[]{:S(2)}, u32[]{:S(2)}) collective-permute-start(bf16[272,768]{1,0:T(8,128)(2,1)} %collective-permute-done.183), channel_id=1, source_target_pairs={{0,4},{4,0},{1,5},{5,1},{2,6},{6,2},{3,7},{7,3},{8,12},{12,8},{9,1... | collective-permute-start | bytes 1253384 | tf_op jit(solution)/shard_map/cond/branch_18_fun/ppermute | solution.py:25
  86.5 19.1 %all-to-all-start.1 = ((f32[48,1,128]{2,1,0:T(1,128)}), f32[48,1,128]{2,1,0:T(1,128)S(1)}, u32[]{:S(2)}, u32[]{:S(2)}) async-start(f32[48,1,128]{2,1,0:T(1,128)} %broadcast_in_dim.8), calls=%async_computation.1 | async-start | bytes 49152 | tf_op jit(solution)/shard_map/all_to_all | solution.py:157
